TPU v7x, 32 devices: a whole 2x2x4 slice. The times are simulated.
32 devices in a mesh: grp: 4 (over y, core), blk: 8 (over z, x).
Axes of the slice: x: 2, y: 2, z: 4, core: 2. Of those that a mesh axis runs over, the one named last changes fastest.
Arguments:
- hidden_in: bfloat16 [8, 512, 1024], P('blk', 'grp'), may hold values from -6 to 6
- attn_gain: float32 [1024], replicated, may hold values from 0.1 to 1.9
- qkv_weight: bfloat16 [1024, 3, 16, 64], P(None, None, 'grp'), may hold values from -0.09375 to 0.09375
- rel_bias: float32 [32, 16], P(None, 'grp'), may hold values from -4 to 4
- prefix_cache: bfloat16 [8, 256, 2, 16, 64], P('blk', None, None, 'grp'), may hold values from -34 to 34
- prefix_owner: int32 [8], replicated, may hold values from 0 to 7, each once
- req_prefix: int32 [8, 2], replicated, may hold values from 0 to 7
- req_pages: int32 [8, 2], replicated, may hold values from 1 to 12, 16 in all within a row
- page_table: int32 [8, 16], replicated, may hold values from 0 to 15, each once within a row
- proj_weight: bfloat16 [1024, 1024], replicated, may hold values from -0.1875 to 0.1875
- mlp_gain: float32 [1024], replicated, may hold values from 0.1 to 1.9
- in_weight: bfloat16 [1024, 4096], P(None, 'grp'), may hold values from -0.1875 to 0.1875
- out_weight: bfloat16 [4096, 1024], P('grp'), may hold values from -0.09375 to 0.09375
Outputs:
- hidden_out: bfloat16 [8, 512, 1024], P('blk', 'grp')
- suffix_cache: bfloat16 [8, 512, 2, 16, 64], P('blk', None, None, 'grp')
Inputs may be any that keep to these rules, and one draw needn't show every extreme that they name: Prefix p's keys and values are row prefix_owner[p] of prefix_cache; every owner column holds one prefix. `req_pages`: each row sums to 16 and no entry exceeds 12. `page_table`: each row is a permutation of the logical pages of a column.
All inputs are finite; a program needn't handle non-finite values.
Results may differ from a plain program's by a relative error of at most 0.012.
Values may be sent and summed in bfloat16 or wider, within the bound.
A program may use at most 128 MiB of HBM per device.

v0:
```python
import jax
import jax.numpy as jnp
from jax import lax
from jax.sharding import PartitionSpec as P

PAGE = 32


EPSILON = 1e-06
THRESHOLDS = (12, 16, 23, 32, 46, 64, 91)


def rms_scale(values, gain):
    mean_sq = jnp.mean(values * values, axis=-1, keepdims=True)
    return values * lax.rsqrt(mean_sq + EPSILON) * gain


def bucket_of(relative):
    magnitude = jnp.abs(relative)
    steps_up = jnp.zeros(relative.shape, jnp.int32)
    for limit in THRESHOLDS:
        steps_up = steps_up + (magnitude >= limit).astype(jnp.int32)
    bucket = jnp.where(magnitude < 8, magnitude, jnp.minimum(8 + steps_up, 15))
    return bucket + 16 * (relative > 0).astype(jnp.int32)


def token_meta(pages_row, lengths_row, page_size, prefix_len):
    inclusive = jnp.cumsum(lengths_row, dtype=jnp.int32)
    exclusive = inclusive - lengths_row
    request = jnp.sum(
        (pages_row[:, None] >= inclusive[None, :]).astype(jnp.int32), axis=1, dtype=jnp.int32
    )
    slot_ids = jnp.arange(lengths_row.shape[0], dtype=jnp.int32)
    start = jnp.sum(
        jnp.where(request[:, None] == slot_ids[None, :], exclusive[None, :], 0),
        axis=1,
        dtype=jnp.int32,
    )
    offsets = (pages_row - start) * page_size + prefix_len
    within = jnp.arange(page_size, dtype=jnp.int32)
    positions = (offsets[:, None] + within[None, :]).reshape(-1)
    requests = jnp.broadcast_to(request[:, None], (request.shape[0], page_size)).reshape(-1)
    return (requests, positions)


def attend_block(queries, key_rows, value_rows, query_req, query_pos, key_req, key_pos, rel_bias):
    scores = jnp.einsum("qhd,khd->hqk", queries, key_rows, preferred_element_type=jnp.float32)
    bucket = bucket_of(key_pos[None, :] - query_pos[:, None])
    bias_add = jnp.zeros(scores.shape, jnp.float32)
    for bucket_id in range(rel_bias.shape[0]):
        bias_add = jnp.where(
            (bucket == bucket_id)[None], rel_bias[bucket_id][:, None, None], bias_add
        )
    allowed = (key_req[None, :] == query_req[:, None])[None]
    scores = jnp.where(allowed, scores + bias_add, -1e30)
    row_max = jnp.max(scores, axis=-1, keepdims=True)
    weights = jnp.exp(scores - row_max)
    weights = (weights / jnp.sum(weights, axis=-1, keepdims=True)).astype(jnp.bfloat16)
    return jnp.einsum(
        "hqk,khd->qhd", weights, value_rows, preferred_element_type=jnp.float32
    ).astype(jnp.bfloat16)


def shards(
    hidden_in,
    attn_gain,
    qkv_weight,
    rel_bias,
    prefix_cache,
    prefix_owner,
    req_prefix,
    req_pages,
    page_table,
    proj_weight,
    mlp_gain,
    in_weight,
    out_weight,
):
    width = hidden_in.shape[2]
    heads_dev = qkv_weight.shape[2]
    head_dim = qkv_weight.shape[3]
    inner = heads_dev * head_dim
    residual = hidden_in[0].astype(jnp.float32)
    normed = rms_scale(residual, attn_gain).astype(jnp.bfloat16)
    qkv_flat = qkv_weight.reshape(width, 3 * inner)
    projected = jnp.dot(
        lax.all_gather(normed, "grp", axis=0, tiled=True),
        qkv_flat,
        preferred_element_type=jnp.float32,
    ).astype(jnp.bfloat16)
    column_tok = projected.shape[0]
    projected = projected.reshape(column_tok, 3, heads_dev, head_dim)
    suffix_cache = projected[:, 1:3][None]
    column = lax.axis_index("blk")
    requests_col = req_prefix.shape[1]
    prefix_ids = jnp.arange(prefix_owner.shape[0], dtype=jnp.int32)
    owner_cols = jnp.sum(
        jnp.where(
            req_prefix[:, :, None] == prefix_ids[None, None, :], prefix_owner[None, None, :], 0
        ),
        axis=2,
        dtype=jnp.int32,
    )
    my_cols = lax.dynamic_index_in_dim(owner_cols, column, 0, keepdims=False)
    prefix_len = prefix_cache.shape[1]
    slot_width = 2 * inner
    local_slot = prefix_cache.reshape(prefix_len, slot_width)
    gathered = lax.all_gather(local_slot[None], "blk", axis=0, tiled=True)
    prefix_rows = jnp.take(gathered, my_cols, axis=0)
    prefix_rows = prefix_rows.reshape(requests_col * prefix_len, 2, heads_dev, head_dim)
    key_rows = jnp.concatenate([prefix_rows[:, 0], projected[:, 1]], axis=0)
    value_rows = jnp.concatenate([prefix_rows[:, 1], projected[:, 2]], axis=0)
    pages_row = lax.dynamic_index_in_dim(page_table, column, 0, keepdims=False)
    lengths_row = lax.dynamic_index_in_dim(req_pages, column, 0, keepdims=False)
    query_req, query_pos = token_meta(pages_row, lengths_row, PAGE, prefix_len)
    slot_ids = jnp.arange(requests_col, dtype=jnp.int32)
    key_req = jnp.concatenate([jnp.repeat(slot_ids, prefix_len), query_req])
    key_pos = jnp.concatenate(
        [jnp.tile(jnp.arange(prefix_len, dtype=jnp.int32), requests_col), query_pos]
    )
    block_rows = min(512, column_tok)
    block_count = column_tok // block_rows

    def one_block(operands):
        block_q, block_req, block_pos = operands
        return attend_block(
            block_q, key_rows, value_rows, block_req, block_pos, key_req, key_pos, rel_bias
        )

    attended = lax.map(
        one_block,
        (
            projected[:, 0].reshape(block_count, block_rows, heads_dev, head_dim),
            query_req.reshape(block_count, block_rows),
            query_pos.reshape(block_count, block_rows),
        ),
    )
    attended = attended.reshape(1, column_tok, inner)
    token_heads = lax.all_to_all(attended, "grp", split_axis=1, concat_axis=2, tiled=True)[0]
    mixed = residual + jnp.dot(token_heads, proj_weight, preferred_element_type=jnp.float32)
    normed_mlp = rms_scale(mixed, mlp_gain).astype(jnp.bfloat16)
    activated = jax.nn.relu(
        jnp.dot(
            lax.all_gather(normed_mlp, "grp", axis=0, tiled=True),
            in_weight,
            preferred_element_type=jnp.float32,
        )
    ).astype(jnp.bfloat16)
    summed = lax.psum_scatter(
        jnp.dot(activated, out_weight, preferred_element_type=jnp.float32).astype(jnp.bfloat16),
        "grp",
        scatter_dimension=0,
        tiled=True,
    ).astype(jnp.float32)
    hidden_out = (mixed + summed).astype(jnp.bfloat16)[None]
    return (hidden_out, suffix_cache)


def solution(mesh):
    return jax.shard_map(
        shards,
        mesh=mesh,
        in_specs=(
            P("blk", "grp", None),
            P(),
            P(None, None, "grp", None),
            P(None, "grp"),
            P("blk", None, None, "grp", None),
            P(),
            P(),
            P(),
            P(),
            P(),
            P(),
            P(None, "grp"),
            P("grp", None),
        ),
        out_specs=(P("blk", "grp", None), P("blk", None, None, "grp", None)),
        check_vma=False,
    )
```

profile of v0, /device:TPU:0, one launch (start us, length us, event | category | flops | bytes accessed | tf_op | source)
XLA Modules:
  0.0 208.7 jit_solution(3867273368891614869)
XLA Ops:
  7.2 1.2 fusion.11
  8.5 1.8 fusion.13
  10.3 1.8 copy.46
  12.2 0.9 select_reduce_fusion
  13.1 0.9 dynamic-slice_reduce_fusion
  14.0 1.9 slice_reduce_fusion.31
  15.9 1.6 slice_reduce_fusion.30
  19.7 1.2 broadcast_compare_fusion.32
  20.9 17.4 %broadcast_compare_fusion.25 = (pred[512,1024]{1,0:T(8,128)(4,1)}, pred[512,1024]{1,0:T(8,128)(4,1)}, pred[512,1024]{1,0:T(8,128)(4,1)}, pred[512,1024]{1,0:T(8,...) fusion(s32[512]{0:T(512)S(1)} %add.896, ...), kind=kLoop, calls=%fused_computation.47 | loop fusion | flops 31981568 | bytes 16783360 | tf_op jit(solution)/shard_map/while/body/eval_jaxpr/eq | solution.py:52
  38.3 3.7 %convolution_convert_fusion.1 = bf16[512,768]{1,0:T(8,128)(2,1)} fusion(bf16[512,1024]{1,0:T(8,128)(2,1)} %all-gather.6.cloned.1.call-done, bf16[1024,768]{0,1:T(8,128)(2,1)} %bitcast.76), kind=kOutput, calls=%fused_computation.19 | convolution fusion | flops 805699584 | bytes 3407872 | tf_op jit(solution)/shard_map/dot_general | solution.py:86
  42.1 1.4 copy.48
  43.5 0.8 slice_bitcast_fusion.5
  44.3 37.0 %all-gather.4.cloned.1.call-done = bf16[8,256,512]{2,1,0:T(8,128)(2,1)} async-done(((bf16[1,256,512]{2,1,0:T(8,128)(2,1)}), bf16[8,256,512]{2,1,0:T(8,128)(2,1)}) %all-gather.4.cloned.1.call-update) | async-done | bytes 2097168 | tf_op jit(solution)/shard_map/all_gather | solution.py:108
  81.3 2.2 %gather_fusion = bf16[2,256,512]{2,1,0:T(8,128)(2,1)S(1)} fusion(bf16[8,256,512]{2,1,0:T(8,128)(2,1)} %all-gather.4.cloned.1.call-done, s32[1024]{0:T(1024)S(1)} %pad_clamp_fusion), kind=kCustom, calls=%fused_computation | custom fusion | bytes 1048584 | tf_op jit(solution)/shard_map/jit(_take)/gather | solution.py:109
  83.5 1.1 copy.47
  84.6 1.4 gather.7
  86.1 29.9 %add_select_fusion = f32[4,512,1024]{2,1,0:T(8,128)} fusion(f32[4]{0:T(128)S(1)} %get-tuple-element.62, f32[4]{0:T(128)S(1)} %get-tuple-element.63, f32[4]{0:T(128)S(1)} %get-tuple-element.23, f32[4]{0:T(128)S(1)} %get-tuple-element.24, f32[4]{0:T(128)S(1)} %get-tuple-element.25, f32[4]{0:T(128)S(1)} %get-tuple-element.26, f32[4]{0:T(128)S(1)} %get-tuple-element.27, ...), kind=kOutput, calls=%fused_computation.4 | convolution fusion | flops 340787200 | bytes 26492928 | tf_op jit(solution)/shard_map/while/body/eval_jaxpr/qhd,khd->hqk/dot_general | solution.py:47
  116.0 7.5 %fusion.30 = f32[4,512]{1,0:T(4,128)S(1)} fusion(f32[4,512,1024]{2,1,0:T(8,128)} %add_select_fusion), kind=kOutput, calls=%fused_computation.138 | output fusion | flops 4195327 | bytes 8396800 | tf_op jit(solution)/shard_map/while/body/eval_jaxpr/sub | solution.py:57
  123.5 10.5 %fusion.10 = bf16[4,64,512]{2,1,0:T(8,128)(2,1)} fusion(f32[4,512]{1,0:T(4,128)S(1)} %fusion.30, bf16[512,4,64]{0,2,1:T(8,128)(2,1)S(1)} %copy-done.1, bf16[512,4,64]{0,2,1:T(8,128)(2,1)S(1)} %get-tuple-element.66, f32[4,512,1024]{2,1,0:T(8,128)} %add_select_fusion), kind=kOutput, calls=%fused_computation.21 | convolution fusion | flops 275909632 | bytes 9183232 | tf_op jit(solution)/shard_map/while/body/eval_jaxpr/hqk,khd->qhd/dot_general | solution.py:59
  134.0 1.3 copy.50
  135.8 2.9 %reduce.67 = bf16[512,256]{1,0:T(8,128)(2,1)} reduce(bf16[512,1,256]{2,1,0:T(2,128)(2,1)S(1)} %bitcast.69, bf16[]{:T(256)} %broadcast.2960), dimensions={1}, to_apply=%bitcast.52.reduce_sub_computation | reduce | bytes 524290
  138.8 1.0 reshape.1101
  139.8 9.1 %all_to_all.15 = bf16[4,2,16384]{2,1,0:T(2,128)(2,1)} all-to-all(bf16[4,2,16384]{2,1,0:T(2,128)(2,1)S(1)} %reshape.1101), channel_id=1, replica_groups=mesh['grp'=4,'blk'=8] {'grp'}, dimensions={0} | all-to-all | bytes 524288 | tf_op jit(solution)/shard_map/all_to_all | solution.py:139
  148.9 1.2 reshape.1102
  150.8 1.8 copy.51
  152.6 2.2 %multiply_reduce_fusion = (f32[128]{0:T(128)S(1)}, f32[128,1024]{1,0:T(8,128)S(1)}) fusion(bf16[128,1024]{0,1:T(8,128)(2,1)} %bitcast.71, bf16[1024,1024]{1,0:T(8,128)(2,1)} %param.22, bf16[1,128,1024]{2,1,0:T(8,128)(2,1)} %param.13), kind=kOutput, calls=%fused_computation.69 | convolution fusion | flops 268959616 | bytes 3146240 | tf_op jit(solution)/shard_map/dot_general | solution.py:140
  154.8 0.8 multiply_convert_fusion
  155.7 14.4 %all-gather.8.cloned.1.call-done = bf16[512,1024]{1,0:T(8,128)(2,1)} async-done(((bf16[128,1024]{1,0:T(8,128)(2,1)}), bf16[512,1024]{1,0:T(8,128)(2,1)}) %all-gather.8.cloned.1.call-update) | async-done | bytes 1048592 | tf_op jit(solution)/shard_map/all_gather | solution.py:144
  170.1 5.2 %convolution_convert_fusion = bf16[512,1024]{1,0:T(8,128)(2,1)} fusion(bf16[1024,1024]{1,0:T(8,128)(2,1)S(1)} %copy-done, bf16[512,1024]{1,0:T(8,128)(2,1)} %all-gather.8.cloned.1.call-done, bf16[1024,1024]{1,0:T(8,128)(2,1)} %param.24), kind=kOutput, calls=%fused_computation.18 | convolution fusion | flops 2149056512 | bytes 6291456 | tf_op jit(solution)/shard_map/dot_general | solution.py:150
  175.4 0.8 slice_bitcast_fusion
  176.2 24.2 %reduce-scatter.2.cloned.1.call-done = bf16[128,1024]{1,0:T(8,128)(2,1)} async-done(((bf16[512,1024]{1,0:T(8,128)(2,1)}), bf16[128,1024]{1,0:T(8,128)(2,1)}) %reduce-scatter.2.cloned.1.call-update) | async-done | bytes 262160 | tf_op jit(solution)/shard_map/reduce_scatter | solution.py:149
  200.4 1.7 fusion.20
  (43 shorter events, 3.9 us)
Async XLA Ops:
  7.2 163.0 %copy-start = (bf16[1024,1024]{1,0:T(8,128)(2,1)S(1)}, bf16[1024,1024]{1,0:T(8,128)(2,1)}, u32[]{:S(2)}) copy-start(bf16[1024,1024]{1,0:T(8,128)(2,1)} %param.25) | copy-start | bytes 6291460
  7.2 31.1 %all-gather.6.cloned.1.call-start = ((), (), s32[]{:S(2)}) async-start(), calls=%async_computation.3 | async-start | bytes 1310720 | tf_op jit(solution)/shard_map/all_gather | solution.py:87
  10.3 71.0 %all-gather.4.cloned.1.call-start = ((), (), s32[]{:S(2)}) async-start(), calls=%async_computation.2 | async-start | bytes 2359296 | tf_op jit(solution)/shard_map/all_gather | solution.py:108
  12.2 158.0 %all-gather.8.cloned.1.call-start = ((), (), s32[]{:S(2)}) async-start(), calls=%async_computation.4 | async-start | bytes 1310720 | tf_op jit(solution)/shard_map/all_gather | solution.py:144
  116.0 7.5 %copy-start.1 = (bf16[512,4,64]{0,2,1:T(8,128)(2,1)S(1)}, bf16[512,4,64]{0,2,1:T(8,128)(2,1)}, u32[]{:S(2)}) copy-start(bf16[512,4,64]{0,2,1:T(8,128)(2,1)} %get-tuple-element.64) | copy-start | bytes 786436
  150.1 4.8 %copy-start.2 = (f32[1024]{0:T(1024)S(1)}, f32[1024]{0:T(1024)}, u32[]{:S(2)}) copy-start(f32[1024]{0:T(1024)} %param.23) | copy-start | bytes 12292
  155.7 44.8 %reduce-scatter.2.cloned.1.call-start = ((), (), s32[]{:S(2)}) async-start(), calls=%async_computation.5 | async-start | bytes 1310720 | tf_op jit(solution)/shard_map/reduce_scatter | solution.py:149
Sparse Core Ops, SparseCore 0:
  10.4 19.4 all-gather.5
  32.0 49.2 all-gather.3
  155.8 14.2 all-gather.7
  175.5 24.8 reduce-scatter.1
where the time goes:
time: 209 us
  waiting for transfers between devices  75.7 us (36%)
  matrix products  51.6 us (25%)
  other arithmetic  36.6 us (18%)
  local copies, waits for them, and re-layouts  21.6 us (10%)
  between operations  13.9 us (7%)
  blocking collectives  9.1 us (4%)
    all_gather x1, waiting for transfers between devices, shards(): gathered = lax.all_gather(local_slot[None], 'blk', axis=0, tiled=True)  37 us
    dot_general x1, matrix products, attend_block(): jnp.einsum('qhd,khd->hqk', queries, key_rows, preferred_element_type=jnp....  29.9 us
    reduce_scatter x1, waiting for transfers between devices, shards(): lax.psum_scatter(jnp.dot(activated, out_weight, preferred_element_type=jn...  24.2 us
    eq x1, other arithmetic, attend_block(): bucket == bucket_id  17.4 us
    all_gather x1, waiting for transfers between devices, shards(): lax.all_gather(normed_mlp, 'grp', axis=0, tiled=True)  14.4 us
    dot_general x1, matrix products, attend_block(): jnp.einsum('hqk,khd->qhd', weights, value_rows, preferred_element_type=jn...  10.5 us
    all_to_all x1, blocking collectives, shards(): lax.all_to_all(attended, 'grp', split_axis=1, concat_axis=2, tiled=True)[0]  9.1 us
    sub x1, other arithmetic, attend_block(): weights = jnp.exp(scores - row_max)  7.51 us
  transfers between devices with their start and end apart: 4, of which 3 were waited for; matrix products, arithmetic and copies ran while one was open for 17% of the time, Pallas kernels for 0%

commit v1 on v0

--- a/solution.py
+++ b/solution.py
@@ -1,6 +1,8 @@
 import jax
 import jax.numpy as jnp
 from jax import lax
+from jax.experimental import pallas as pl
+from jax.experimental.pallas import tpu as pltpu
 from jax.sharding import PartitionSpec as P
 
 PAGE = 32
@@ -25,7 +27,10 @@
 
 
 def token_meta(pages_row, lengths_row, page_size, prefix_len):
-    inclusive = jnp.cumsum(lengths_row, dtype=jnp.int32)
+    order = jnp.arange(lengths_row.shape[0], dtype=jnp.int32)
+    inclusive = jnp.sum(
+        jnp.where(order[None, :] <= order[:, None], lengths_row[None, :], 0), axis=1, dtype=jnp.int32
+    )
     exclusive = inclusive - lengths_row
     request = jnp.sum(
         (pages_row[:, None] >= inclusive[None, :]).astype(jnp.int32), axis=1, dtype=jnp.int32
@@ -106,7 +111,12 @@
     slot_width = 2 * inner
     local_slot = prefix_cache.reshape(prefix_len, slot_width)
     gathered = lax.all_gather(local_slot[None], "blk", axis=0, tiled=True)
-    prefix_rows = jnp.take(gathered, my_cols, axis=0)
+    prefix_rows = jnp.stack(
+        [
+            lax.dynamic_index_in_dim(gathered, my_cols[k], 0, keepdims=False)
+            for k in range(requests_col)
+        ]
+    )
     prefix_rows = prefix_rows.reshape(requests_col * prefix_len, 2, heads_dev, head_dim)
     key_rows = jnp.concatenate([prefix_rows[:, 0], projected[:, 1]], axis=0)
     value_rows = jnp.concatenate([prefix_rows[:, 1], projected[:, 2]], axis=0)
@@ -156,9 +166,392 @@
     return (hidden_out, suffix_cache)
 
 
+MESH = pl.DeviceIdType.MESH
+TILE = 128
+
+
+def remote(src, dst, send, recv, where):
+    return pltpu.make_async_remote_copy(
+        src_ref=src, dst_ref=dst, send_sem=send, recv_sem=recv, device_id=where, device_id_type=MESH
+    )
+
+
+def grp_places():
+    me = lax.axis_index("grp")
+    y, core = me // 2, me % 2
+    return me, y * 2 + 1 - core, (1 - y) * 2 + core, (1 - y) * 2 + 1 - core
+
+
+def rms_rows(values, gain):
+    mean_sq = jnp.mean(values * values, axis=-1, keepdims=True)
+    return (values * lax.rsqrt(mean_sq + EPSILON) * gain).astype(jnp.bfloat16)
+
+
+def qkv_kernel(
+    hidden, gain, weight, prefix, owner, req_prefix,
+    qkv, picked,
+    states, slots, g_send, g_recv, r_send, r_recv, l_send, l_recv, x_send, x_recv, own_sem,
+):
+    me, mate, across, diag = grp_places()
+    blk = lax.axis_index("blk")
+    z, x = blk // 2, blk % 2
+    other = z * 2 + 1 - x
+    mine = pltpu.make_async_copy(prefix, slots.at[blk], own_sem)
+    mine.start()
+    barrier = pltpu.get_barrier_semaphore()
+    for place in ({"grp": mate}, {"grp": across}, {"blk": other},
+                  {"blk": (z + 1) % 4 * 2 + x}, {"blk": (z + 3) % 4 * 2 + x}):
+        pl.semaphore_signal(barrier, inc=1, device_id=place, device_id_type=MESH)
+    pl.semaphore_wait(barrier, 5)
+    mine.wait()
+
+    def up(slot, s):
+        ref = slots.at[slot * 2 + x]
+        return remote(ref, ref, r_send.at[s], r_recv.at[s], {"blk": (z + 1) % 4 * 2 + x})
+
+    def down(slot, s):
+        ref = slots.at[slot * 2 + x]
+        return remote(ref, ref, l_send.at[s], l_recv.at[s], {"blk": (z + 3) % 4 * 2 + x})
+
+    def over(slot, side):
+        ref = slots.at[slot * 2 + side]
+        return remote(ref, ref, x_send.at[slot], x_recv.at[slot], {"blk": other})
+
+    def hop(s):
+        @pl.when((z < 3) & (z >= s))
+        def _():
+            up(z - s, s).start()
+
+        @pl.when((z > 0) & (z + s <= 3))
+        def _():
+            down(z + s, s).start()
+
+    def land(s):
+        @pl.when(z >= s + 1)
+        def _():
+            up(z - 1 - s, s).wait_recv()
+
+        @pl.when(z + s + 1 <= 3)
+        def _():
+            down(z + 1 + s, s).wait_recv()
+
+        if s < 2:
+            hop(s + 1)
+
+        @pl.when(z >= s + 1)
+        def _():
+            over(z - 1 - s, x).start()
+
+        @pl.when(z + s + 1 <= 3)
+        def _():
+            over(z + 1 + s, x).start()
+
+    hop(0)
+    over(z, x).start()
+    states[me] = rms_rows(hidden[...].astype(jnp.float32), gain[...])
+    to_mate = remote(states.at[me], states.at[me], g_send.at[0], g_recv.at[0], {"grp": mate})
+    to_across = remote(states.at[me], states.at[me], g_send.at[1], g_recv.at[1], {"grp": across})
+    to_across.start()
+    to_mate.start()
+
+    def project(place):
+        rows = pl.ds(pl.multiple_of(place * TILE, TILE), TILE)
+        qkv[rows, :] = jnp.dot(
+            states[place], weight[...], preferred_element_type=jnp.float32
+        ).astype(jnp.bfloat16)
+
+    project(me)
+    remote(states.at[mate], states.at[mate], g_send.at[0], g_recv.at[0], {"grp": mate}).wait_recv()
+    project(mate)
+    remote(states.at[across], states.at[across], g_send.at[1], g_recv.at[1], {"grp": across}).wait_recv()
+    onward = remote(states.at[across], states.at[across], g_send.at[2], g_recv.at[2], {"grp": mate})
+    onward.start()
+    land(0)
+    project(across)
+    remote(states.at[diag], states.at[diag], g_send.at[2], g_recv.at[2], {"grp": mate}).wait_recv()
+    project(diag)
+    land(1)
+    land(2)
+    for slot in range(4):
+        over(slot, 1 - x).wait_recv()
+    for k in range(2):
+        picked[k] = slots[owner[req_prefix[blk, k]]]
+    to_mate.wait_send()
+    to_across.wait_send()
+    onward.wait_send()
+    for s in range(3):
+        @pl.when((z < 3) & (z >= s))
+        def _():
+            up(z - s, s).wait_send()
+
+        @pl.when((z > 0) & (z + s <= 3))
+        def _():
+            down(z + s, s).wait_send()
+    for slot in range(4):
+        over(slot, x).wait_send()
+
+
+def attend_kernel(qkv, picked, pages, lengths, rel_bias, out, ordered, result, tiles, shifted):
+    blk = lax.axis_index("blk")
+    tokens, inner = out.shape
+    page_count = tokens // PAGE
+    heads = rel_bias.shape[1]
+    dim = inner // heads
+    split = lengths[blk, 0] * PAGE
+    row = lax.broadcasted_iota(jnp.int32, (TILE, TILE), 0)
+    col = lax.broadcasted_iota(jnp.int32, (TILE, TILE), 1)
+
+    @pl.loop(1, 4)
+    def _(d):
+        bucket = bucket_of((d - 2) * TILE + col - row)
+        sums = [jnp.zeros((TILE, TILE), jnp.float32)] * heads
+        for b in range(rel_bias.shape[0]):
+            here = bucket == b
+            sums = [jnp.where(here, rel_bias[b, h], sums[h]) for h in range(heads)]
+        for h in range(heads):
+            tiles[h, d] = sums[h]
+
+    for h in range(heads):
+        tiles[h, 0] = jnp.full((TILE, TILE), rel_bias[15, h], jnp.float32)
+        tiles[h, 4] = jnp.full((TILE, TILE), rel_bias[31, h], jnp.float32)
+        shifted[h] = jnp.full((2 * tokens, TILE), rel_bias[15, h], jnp.float32)
+        shifted[h, tokens:tokens + TILE] = tiles[h, 1]
+
+    @pl.loop(0, page_count)
+    def _(logical):
+        physical = jnp.int32(0)
+        for j in range(page_count):
+            physical = physical + jnp.where(pages[blk, j] == logical, j, 0)
+        ordered[pl.ds(pl.multiple_of(logical * PAGE, PAGE), PAGE), :] = qkv[
+            pl.ds(pl.multiple_of(physical * PAGE, PAGE), PAGE), :
+        ]
+
+    blocks = tokens // TILE
+    key_late = lax.broadcasted_iota(jnp.int32, (TILE, tokens), 1) >= split
+
+    @pl.loop(0, blocks)
+    def _(i):
+        rows = pl.ds(pl.multiple_of(i * TILE, TILE), TILE)
+        number = i * TILE + lax.broadcasted_iota(jnp.int32, (TILE, tokens), 0)
+        allowed = (number >= split) == key_late
+        late = i * TILE + lax.broadcasted_iota(jnp.int32, (TILE, 2 * TILE), 0) >= split
+        shift = pl.multiple_of(tokens + i * TILE - split, PAGE)
+        contract = (((1,), (1,)), ((), ()))
+        for h in range(heads):
+            at = slice(h * dim, (h + 1) * dim)
+            key_at = slice(inner + h * dim, inner + (h + 1) * dim)
+            value_at = slice(2 * inner + h * dim, 2 * inner + (h + 1) * dim)
+            q = ordered[rows, at]
+
+            def against(keys):
+                return lax.dot_general(q, keys, contract, preferred_element_type=jnp.float32)
+
+            own = against(ordered[:, key_at])
+            bias = jnp.concatenate(
+                [tiles[h, jnp.clip(j - i, -2, 2) + 2] for j in range(blocks)], axis=1
+            )
+            own = jnp.where(allowed, own + bias, -1e30)
+            far = jnp.full((TILE, TILE), rel_bias[15, h], jnp.float32)
+            early = jnp.concatenate([far, tiles[h, jnp.maximum(1 - i, 0)]], axis=1)
+            later = jnp.concatenate([far, shifted[h, pl.ds(shift, TILE), :]], axis=1)
+            before = jnp.where(
+                late, against(picked[1, :, at]) + later, against(picked[0, :, at]) + early
+            )
+            top = jnp.maximum(
+                jnp.max(own, axis=1, keepdims=True), jnp.max(before, axis=1, keepdims=True)
+            )
+            own = jnp.exp(own - top)
+            before = jnp.exp(before - top)
+            total = jnp.sum(own, axis=1, keepdims=True) + jnp.sum(before, axis=1, keepdims=True)
+            summed = jnp.dot(
+                own.astype(jnp.bfloat16), ordered[:, value_at], preferred_element_type=jnp.float32
+            )
+            for k in range(2):
+                part = jnp.where(late == (k == 1), before, 0.0).astype(jnp.bfloat16)
+                summed = summed + jnp.dot(
+                    part, picked[k, :, key_at], preferred_element_type=jnp.float32
+                )
+            result[rows, at] = (summed / total).astype(jnp.bfloat16)
+
+    @pl.loop(0, page_count)
+    def _(j):
+        out[pl.ds(pl.multiple_of(j * PAGE, PAGE), PAGE), :] = result[
+            pl.ds(pl.multiple_of(pages[blk, j] * PAGE, PAGE), PAGE), :
+        ]
+
+
+def mlp_kernel(
+    hidden, attended, proj_hbm, gain, in_hbm, out_hbm,
+    final,
+    proj, in_w, out_w, heads_in, states, mixed, total, leaving, arriving,
+    w_sem, a_send, a_recv, g_send, g_recv, s_send, s_recv,
+):
+    me, mate, across, diag = grp_places()
+    loads = [
+        pltpu.make_async_copy(a, b, w_sem.at[k])
+        for k, (a, b) in enumerate(((proj_hbm, proj), (in_hbm, in_w), (out_hbm, out_w)))
+    ]
+    for load in loads:
+        load.start()
+    barrier = pltpu.get_barrier_semaphore()
+    for place in (mate, across, diag):
+        pl.semaphore_signal(barrier, inc=1, device_id={"grp": place}, device_id_type=MESH)
+    pl.semaphore_wait(barrier, 3)
+
+    def rows_of(place):
+        return pl.ds(pl.multiple_of(place * TILE, TILE), TILE)
+
+    def share_out(k, place):
+        return remote(
+            attended.at[rows_of(place), :], heads_in.at[me], a_send.at[k], a_recv.at[k], {"grp": place}
+        )
+
+    def share_in(k, place):
+        return remote(
+            attended.at[rows_of(place), :], heads_in.at[place], a_send.at[k], a_recv.at[k], {"grp": place}
+        )
+
+    peers = ((1, across), (2, diag), (0, mate))
+    for k, place in peers:
+        share_out(k, place).start()
+    depth = attended.shape[1]
+
+    def mix(block, place):
+        return jnp.dot(
+            block,
+            proj[pl.ds(pl.multiple_of(place * depth, depth), depth), :],
+            preferred_element_type=jnp.float32,
+        )
+
+    loads[0].wait()
+    mixed[...] = hidden[...].astype(jnp.float32) + mix(attended[rows_of(me), :], me)
+    for k, place in ((0, mate), (1, across), (2, diag)):
+        share_in(k, place).wait_recv()
+        mixed[...] += mix(heads_in[place], place)
+    states[me] = rms_rows(mixed[...], gain[...])
+    to_mate = remote(states.at[me], states.at[me], g_send.at[0], g_recv.at[0], {"grp": mate})
+    to_across = remote(states.at[me], states.at[me], g_send.at[1], g_recv.at[1], {"grp": across})
+    to_across.start()
+    to_mate.start()
+    loads[1].wait()
+    loads[2].wait()
+
+    def share(place):
+        hidden_units = jnp.dot(states[place], in_w[...], preferred_element_type=jnp.float32)
+        activated = jnp.maximum(hidden_units, 0.0).astype(jnp.bfloat16)
+        return jnp.dot(activated, out_w[...], preferred_element_type=jnp.float32)
+
+    def give(k, place):
+        return remote(leaving.at[k], arriving.at[k], s_send.at[k], s_recv.at[k], {"grp": place})
+
+    total[...] = share(me)
+    remote(states.at[mate], states.at[mate], g_send.at[0], g_recv.at[0], {"grp": mate}).wait_recv()
+    leaving[0] = share(mate).astype(jnp.bfloat16)
+    give(0, mate).start()
+    total[...] += mixed[...]
+    remote(states.at[across], states.at[across], g_send.at[1], g_recv.at[1], {"grp": across}).wait_recv()
+    onward = remote(states.at[across], states.at[across], g_send.at[2], g_recv.at[2], {"grp": mate})
+    onward.start()
+    mixed[...] = share(across)
+    remote(states.at[diag], states.at[diag], g_send.at[2], g_recv.at[2], {"grp": mate}).wait_recv()
+    leaving[1] = share(diag).astype(jnp.bfloat16)
+    give(1, mate).start()
+    give(1, mate).wait_recv()
+    leaving[2] = (mixed[...] + arriving[1].astype(jnp.float32)).astype(jnp.bfloat16)
+    give(2, across).start()
+    give(0, mate).wait_recv()
+    total[...] += arriving[0].astype(jnp.float32)
+    give(2, across).wait_recv()
+    final[...] = (total[...] + arriving[2].astype(jnp.float32)).astype(jnp.bfloat16)
+    for k, place in peers:
+        share_out(k, place).wait_send()
+    to_mate.wait_send()
+    to_across.wait_send()
+    onward.wait_send()
+    give(0, mate).wait_send()
+    give(1, mate).wait_send()
+    give(2, across).wait_send()
+
+
+VMEM = pl.BlockSpec(memory_space=pltpu.VMEM)
+SMEM = pl.BlockSpec(memory_space=pltpu.SMEM)
+HBM = pl.BlockSpec(memory_space=pl.ANY)
+LIMIT = 48 * 2**20
+
+
+def fused_shards(
+    hidden_in, attn_gain, qkv_weight, rel_bias, prefix_cache, prefix_owner, req_prefix,
+    req_pages, page_table, proj_weight, mlp_gain, in_weight, out_weight,
+):
+    hidden = hidden_in[0]
+    local, width = hidden.shape
+    heads, dim = qkv_weight.shape[2:]
+    inner = heads * dim
+    tokens = 4 * local
+    plen = prefix_cache.shape[1]
+    dma = pltpu.SemaphoreType.DMA
+    bf16, f32 = jnp.bfloat16, jnp.float32
+    qkv, picked = pl.pallas_call(
+        qkv_kernel,
+        out_shape=(
+            jax.ShapeDtypeStruct((tokens, 3 * inner), bf16),
+            jax.ShapeDtypeStruct((2, plen, 2 * inner), bf16),
+        ),
+        in_specs=[VMEM] * 4 + [SMEM] * 2,
+        out_specs=(VMEM, VMEM),
+        scratch_shapes=[
+            pltpu.VMEM((4, local, width), bf16),
+            pltpu.VMEM((8, plen, 2 * inner), bf16),
+            dma((3,)), dma((3,)), dma((3,)), dma((3,)), dma((3,)), dma((3,)), dma((4,)), dma((4,)), dma,
+        ],
+        compiler_params=pltpu.CompilerParams(
+            collective_id=0, has_side_effects=True, vmem_limit_bytes=LIMIT
+        ),
+    )(
+        hidden, attn_gain.reshape(1, width), qkv_weight.reshape(width, 3 * inner),
+        prefix_cache.reshape(plen, 2 * inner), prefix_owner, req_prefix,
+    )
+    attended = pl.pallas_call(
+        attend_kernel,
+        out_shape=jax.ShapeDtypeStruct((tokens, inner), bf16),
+        in_specs=[VMEM] * 2 + [SMEM] * 3,
+        out_specs=VMEM,
+        scratch_shapes=[
+            pltpu.VMEM((tokens, 3 * inner), bf16),
+            pltpu.VMEM((tokens, inner), bf16),
+            pltpu.VMEM((heads, 5, TILE, TILE), f32),
+            pltpu.VMEM((heads, 2 * tokens, TILE), f32),
+        ],
+        compiler_params=pltpu.CompilerParams(vmem_limit_bytes=LIMIT),
+    )(qkv, picked, page_table, req_pages, rel_bias)
+    hidden_out = pl.pallas_call(
+        mlp_kernel,
+        out_shape=jax.ShapeDtypeStruct((local, width), bf16),
+        in_specs=[VMEM, VMEM, HBM, VMEM, HBM, HBM],
+        out_specs=VMEM,
+        scratch_shapes=[
+            pltpu.VMEM(proj_weight.shape, bf16),
+            pltpu.VMEM(in_weight.shape, bf16),
+            pltpu.VMEM(out_weight.shape, bf16),
+            pltpu.VMEM((4, local, inner), bf16),
+            pltpu.VMEM((4, local, width), bf16),
+            pltpu.VMEM((local, width), f32),
+            pltpu.VMEM((local, width), f32),
+            pltpu.VMEM((3, local, width), bf16),
+            pltpu.VMEM((3, local, width), bf16),
+            dma((3,)), dma((3,)), dma((3,)), dma((3,)), dma((3,)), dma((3,)), dma((3,)),
+        ],
+        compiler_params=pltpu.CompilerParams(
+            collective_id=1, has_side_effects=True, vmem_limit_bytes=LIMIT
+        ),
+    )(hidden, attended, proj_weight, mlp_gain.reshape(1, width), in_weight, out_weight)
+    suffix_cache = qkv[:, inner:].reshape(1, tokens, 2, heads, dim)
+    return hidden_out[None], suffix_cache
+
+
 def solution(mesh):
     return jax.shard_map(
-        shards,
+        fused_shards if (mesh.shape["grp"], mesh.shape["blk"]) == (4, 8) else shards,
         mesh=mesh,
         in_specs=(
             P("blk", "grp", None),

time: 209 us -> 75.4 us (0.36)
  waiting for transfers between devices: 75.7 us -> 0 us
  Pallas kernels: 0 us -> 67.3 us
  matrix products: 51.6 us -> 0 us
  other arithmetic: 36.6 us -> 0 us
  local copies, waits for them, and re-layouts: 21.6 us -> 7.12 us
  between operations: 13.9 us -> 0.79 us
  blocking collectives: 9.1 us -> 0 us
    pallas_call x0 -> x3, Pallas kernels: none -> 67.3 us  [the longest x1 31.9 us: fused_shards(): pl.pallas_call(qkv_kernel, out_shape=(jax.ShapeDtypeStruct((tokens, 3 * i...]
    dot_general x5 -> x0, matrix products: 51.6 us -> none  [the longest x1 29.9 us: attend_block(): jnp.einsum('qhd,khd->hqk', queries, key_rows, preferred_element_type=jnp....]
    all_gather x3 -> x0, waiting for transfers between devices: 51.4 us -> none  [the longest x1 37 us: shards(): gathered = lax.all_gather(local_slot[None], 'blk', axis=0, tiled=True)]
    reduce_scatter x1 -> x0, waiting for transfers between devices: 24.2 us -> none  [shards(): lax.psum_scatter(jnp.dot(activated, out_weight, preferred_element_type=jn...]
    eq x2 -> x0, other arithmetic: 18.5 us -> none  [the longest x1 17.4 us: attend_block(): bucket == bucket_id]
    all_to_all x1 -> x0, blocking collectives: 9.1 us -> none  [shards(): lax.all_to_all(attended, 'grp', split_axis=1, concat_axis=2, tiled=True)[0]]
    sub x1 -> x0, other arithmetic: 7.51 us -> none  [attend_block(): weights = jnp.exp(scores - row_max)]
    gather x3 -> x0, local copies, waits for them, and re-layouts: 4.64 us -> none  [shards(): prefix_rows = jnp.take(gathered, my_cols, axis=0)]
  transfers between devices with their start and end apart: 4 -> 0, of which waited for: 3 -> 0; matrix products, arithmetic and copies ran while one was open for 17% -> 0% of each run, Pallas kernels for 0% -> 0%
where the time goes in v1:
time: 75.4 us; the launch traced here: 75.2 us
  Pallas kernels  67.3 us (89%)
  local copies, waits for them, and re-layouts  7.12 us (9%)
  between operations  0.79 us (1%)
    pallas_call x1, Pallas kernels, fused_shards(): pl.pallas_call(qkv_kernel, out_shape=(jax.ShapeDtypeStruct((tokens, 3 * i...  31.9 us
    pallas_call x1, Pallas kernels, fused_shards(): pl.pallas_call(mlp_kernel, out_shape=jax.ShapeDtypeStruct((local, width),...  24.7 us
    pallas_call x1, Pallas kernels, fused_shards(): pl.pallas_call(attend_kernel, out_shape=jax.ShapeDtypeStruct((tokens, inn...  10.7 us
    unnamed x26, local copies, waits for them, and re-layouts  4.18 us
    reshape x1, local copies, waits for them, and re-layouts, fused_shards(): qkv_weight.reshape(width, 3 * inner)  1.76 us

profile of v1, /device:TPU:0, one launch (start us, length us, event | category | flops | bytes accessed | tf_op | source)
XLA Modules:
  0.0 75.2 jit_solution(2851719906803943613)
XLA Ops:
  0.6 0.0 copy-start.2
  0.6 0.0 copy-start.7
  0.7 0.0 copy-start.9
  0.7 0.0 copy-start.3
  0.7 0.0 copy-start.6
  0.7 1.8 %copy.21.weight = bf16[1024,768]{1,0:T(8,128)(2,1)S(1)} copy(bf16[1024,768]{0,1:T(8,128)(2,1)} %bitcast.12) | data formatting | bytes 3145728 | tf_op jit(solution)/shard_map/reshape | solution.py:511
  2.5 0.0 copy-start.8
  2.5 0.0 copy-start.10
  2.5 0.0 copy-start.4
  2.5 0.0 copy-done.7
  2.5 0.0 copy-start.5
  2.5 0.1 copy.22.prefix
  2.7 0.0 copy-done.9
  2.7 0.1 copy.23.req_prefix
  2.8 0.0 copy-done.2
  2.8 0.0 copy-done.3
  2.8 0.0 copy-done.6
  2.8 31.9 %shard_map.140 = (bf16[512,768]{1,0:T(8,128)(2,1)S(1)}, bf16[2,256,512]{2,1,0:T(8,128)(2,1)S(1)}) custom-call(bf16[128,1024]{1,0:T(8,128)(2,1)S(1)} %bitcast.7, f32[1,1024]{1,0:T(1,128)S(1)} %bitcast.10, bf16[1024,768]{1,0:T(8,128)(2,1)S(1)} %copy.21.weight, bf16[256,512]{1,0:T(8,128)(2,1)S(1)} %copy.22.prefix, s32[8]{0:T(128)S(1)} %copy-done.6, ...), custom_call_target="tpu_custom_call" | custom-call | tf_op jit(solution)/shard_map/pallas_call | solution.py:494
  34.6 0.0 copy-done.8
  34.6 0.1 copy.25.rel_bias
  34.7 0.0 copy-done.10
  34.7 0.1 copy.24.lengths
  34.8 0.0 copy-done.4
  34.8 10.7 %shard_map.141.attended = bf16[512,256]{1,0:T(8,128)(2,1)S(1)} custom-call(bf16[512,768]{1,0:T(8,128)(2,1)S(1)} %get-tuple-element.4.qkv, bf16[2,256,512]{2,1,0:T(8,128)(2,1)S(1)} %get-tuple-element.5.picked, s32[8,16]{1,0:T(8,128)S(1)} %copy-done.4, s32[8,2]{1,0:T(8,128)S(1)} %copy.24.lengths, f32[32,4]{1,0:T(8,128)S(1)} %copy.25.rel_bias), custom_call_target="tpu_custom_call" | custom-call | tf_op jit(solution)/shard_map/pallas_call | solution.py:514
  45.6 0.0 copy-done.5
  45.6 0.0 copy-start
  45.6 1.6 %copy-done = bf16[1024,1024]{1,0:T(8,128)(2,1)S(1)} copy-done((bf16[1024,1024]{1,0:T(8,128)(2,1)S(1)}, bf16[1024,1024]{1,0:T(8,128)(2,1)}, u32[]{:S(2)}) %copy-start) | copy-done | bytes 2097176
  47.2 0.0 copy-start.1
  47.2 1.6 %copy-done.1 = bf16[1024,1024]{1,0:T(8,128)(2,1)S(1)} copy-done((bf16[1024,1024]{1,0:T(8,128)(2,1)S(1)}, bf16[1024,1024]{1,0:T(8,128)(2,1)}, u32[]{:S(2)}) %copy-start.1) | copy-done | bytes 2097176
  48.8 24.7 %shard_map.142 = bf16[128,1024]{1,0:T(8,128)(2,1)S(1)} custom-call(bf16[128,1024]{1,0:T(8,128)(2,1)S(1)} %bitcast.8, bf16[512,256]{1,0:T(8,128)(2,1)S(1)} %shard_map.141.attended, bf16[1024,1024]{1,0:T(8,128)(2,1)S(1)} %copy-done, f32[1,1024]{1,0:T(1,128)S(1)} %bitcast.11, bf16[1024,1024]{1,0:T(8,128)(2,1)S(1)} %copy-done.1, bf16[1024,1024]{1,0:T(8,128)(2,1)} %out_hbm.1), custom_call_target="tpu_custom_call" | custom-call | tf_op jit(solution)/shard_map/pallas_call | solution.py:527
  73.5 1.0 %copy.26 = bf16[512,512]{0,1:T(8,128)(2,1)} copy(bf16[512,512]{1,0:T(8,128)(2,1)S(1)} %slice.3) | data formatting | bytes 1048576 | tf_op jit(solution)/shard_map/slice | solution.py:548
  74.5 0.7 copy.28
  (1 shorter events, 0.0 us)
Async XLA Ops:
  0.6 2.1 %copy-start.2 = (bf16[1,128,1024]{2,1,0:T(8,128)(2,1)S(1)}, bf16[1,128,1024]{2,1,0:T(8,128)(2,1)}, u32[]{:S(2)}) copy-start(bf16[1,128,1024]{2,1,0:T(8,128)(2,1)} %param.13) | copy-start | bytes 786436
  0.6 1.8 %copy-start.7 = (bf16[1,256,2,4,64]{1,4,3,2,0:T(8,128)(2,1)S(1)}, bf16[1,256,2,4,64]{1,4,3,2,0:T(8,128)(2,1)}, u32[]{:S(2)}) copy-start(bf16[1,256,2,4,64]{1,4,3,2,0:T(8,128)(2,1)} %param.17) | copy-start | bytes 786436
  0.7 2.0 %copy-start.9 = (s32[8,2]{0,1:T(2,128)S(1)}, s32[8,2]{0,1:T(2,128)}, u32[]{:S(2)}) copy-start(s32[8,2]{0,1:T(2,128)} %param.19) | copy-start | bytes 196
  0.7 2.1 %copy-start.3 = (f32[1024]{0:T(1024)S(1)}, f32[1024]{0:T(1024)}, u32[]{:S(2)}) copy-start(f32[1024]{0:T(1024)} %param.14) | copy-start | bytes 12292
  0.7 2.1 %copy-start.6 = (s32[8]{0:T(128)S(1)}, s32[8]{0:T(128)}, u32[]{:S(2)}) copy-start(s32[8]{0:T(128)} %owner.1) | copy-start | bytes 100
  2.5 32.2 %copy-start.8 = (f32[32,4]{0,1:T(4,128)S(1)}, f32[32,4]{0,1:T(4,128)}, u32[]{:S(2)}) copy-start(f32[32,4]{0,1:T(4,128)} %param.16) | copy-start | bytes 1540
  2.5 32.3 %copy-start.10 = (s32[8,2]{0,1:T(2,128)S(1)}, s32[8,2]{0,1:T(2,128)}, u32[]{:S(2)}) copy-start(s32[8,2]{0,1:T(2,128)} %param.20) | copy-start | bytes 196
  2.5 32.3 %copy-start.4 = (s32[8,16]{1,0:T(8,128)S(1)}, s32[8,16]{1,0:T(8,128)}, u32[]{:S(2)}) copy-start(s32[8,16]{1,0:T(8,128)} %pages.1) | copy-start | bytes 1540
  2.5 43.1 %copy-start.5 = (f32[1024]{0:T(1024)S(1)}, f32[1024]{0:T(1024)}, u32[]{:S(2)}) copy-start(f32[1024]{0:T(1024)} %param.23) | copy-start | bytes 12292
  45.6 1.6 %copy-start = (bf16[1024,1024]{1,0:T(8,128)(2,1)S(1)}, bf16[1024,1024]{1,0:T(8,128)(2,1)}, u32[]{:S(2)}) copy-start(bf16[1024,1024]{1,0:T(8,128)(2,1)} %proj_hbm.1) | copy-start | bytes 6291460
  47.2 1.6 %copy-start.1 = (bf16[1024,1024]{1,0:T(8,128)(2,1)S(1)}, bf16[1024,1024]{1,0:T(8,128)(2,1)}, u32[]{:S(2)}) copy-start(bf16[1024,1024]{1,0:T(8,128)(2,1)} %in_hbm.1) | copy-start | bytes 6291460

commit v2 on v1

--- a/solution.py
+++ b/solution.py
@@ -542,7 +542,7 @@
             dma((3,)), dma((3,)), dma((3,)), dma((3,)), dma((3,)), dma((3,)), dma((3,)),
         ],
         compiler_params=pltpu.CompilerParams(
-            collective_id=1, has_side_effects=True, vmem_limit_bytes=LIMIT
+            collective_id=1, has_side_effects=True, vmem_limit_bytes=60 * 2**20
         ),
     )(hidden, attended, proj_weight, mlp_gain.reshape(1, width), in_weight, out_weight)
     suffix_cache = qkv[:, inner:].reshape(1, tokens, 2, heads, dim)

time: 75.4 us -> 74.3 us (0.985)
  local copies, waits for them, and re-layouts: 7.12 us -> 4.64 us
  Pallas kernels: 67.3 us -> 68.7 us
    unnamed x26 -> x24, local copies, waits for them, and re-layouts: 4.18 us -> 1.7 us
    pallas_call x1, Pallas kernels: 24.7 us -> 26.1 us  [fused_shards(): pl.pallas_call(mlp_kernel, out_shape=jax.ShapeDtypeStruct((local, width),...]
where the time goes in v2:
time: 74.3 us; the launch traced here: 74.2 us
  Pallas kernels  68.7 us (92%)
  local copies, waits for them, and re-layouts  4.64 us (6%)
  between operations  0.79 us (1%)
    pallas_call x1, Pallas kernels, fused_shards(): pl.pallas_call(qkv_kernel, out_shape=(jax.ShapeDtypeStruct((tokens, 3 * i...  31.9 us
    pallas_call x1, Pallas kernels, fused_shards(): pl.pallas_call(mlp_kernel, out_shape=jax.ShapeDtypeStruct((local, width),...  26.1 us
    pallas_call x1, Pallas kernels, fused_shards(): pl.pallas_call(attend_kernel, out_shape=jax.ShapeDtypeStruct((tokens, inn...  10.7 us
    reshape x1, local copies, waits for them, and re-layouts, fused_shards(): qkv_weight.reshape(width, 3 * inner)  1.76 us
    unnamed x24, local copies, waits for them, and re-layouts  1.7 us

profile of v2, /device:TPU:0, one launch (start us, length us, event | category | flops | bytes accessed | tf_op | source)
XLA Modules:
  0.0 74.2 jit_solution(6469018525103594085)
XLA Ops:
  0.6 0.0 copy-start
  0.6 0.0 copy-start.6
  0.7 0.0 copy-start.8
  0.7 0.0 copy-start.2
  0.7 0.0 copy-start.4
  0.7 1.8 %copy.21.weight = bf16[1024,768]{1,0:T(8,128)(2,1)S(1)} copy(bf16[1024,768]{0,1:T(8,128)(2,1)} %bitcast.10) | data formatting | bytes 3145728 | tf_op jit(solution)/shard_map/reshape | solution.py:511
  2.5 0.0 copy-start.7
  2.5 0.0 copy-start.9
  2.5 0.0 copy-start.3
  2.5 0.0 copy-done.6
  2.5 0.1 copy.22.prefix
  2.6 0.0 copy-done.8
  2.7 0.1 copy.23.req_prefix
  2.7 0.0 copy-done
  2.7 0.0 copy-done.2
  2.7 0.0 copy-done.4
  2.7 31.9 %shard_map.140 = (bf16[512,768]{1,0:T(8,128)(2,1)S(1)}, bf16[2,256,512]{2,1,0:T(8,128)(2,1)S(1)}) custom-call(bf16[128,1024]{1,0:T(8,128)(2,1)S(1)} %bitcast.8, f32[1,1024]{1,0:T(1,128)S(1)} %bitcast.9, bf16[1024,768]{1,0:T(8,128)(2,1)S(1)} %copy.21.weight, bf16[256,512]{1,0:T(8,128)(2,1)S(1)} %copy.22.prefix, s32[8]{0:T(128)S(1)} %copy-done.4, ...), custom_call_target="tpu_custom_call" | custom-call | tf_op jit(solution)/shard_map/pallas_call | solution.py:494
  34.6 0.0 copy-done.7
  34.6 0.1 copy.25.rel_bias
  34.7 0.0 copy-done.9
  34.7 0.1 copy.24.lengths
  34.8 0.0 copy-done.3
  34.8 10.7 %shard_map.141.attended = bf16[512,256]{1,0:T(8,128)(2,1)S(1)} custom-call(bf16[512,768]{1,0:T(8,128)(2,1)S(1)} %get-tuple-element.4.qkv, bf16[2,256,512]{2,1,0:T(8,128)(2,1)S(1)} %get-tuple-element.5.picked, s32[8,16]{1,0:T(8,128)S(1)} %copy-done.3, s32[8,2]{1,0:T(8,128)S(1)} %copy.24.lengths, f32[32,4]{1,0:T(8,128)S(1)} %copy.25.rel_bias), custom_call_target="tpu_custom_call" | custom-call | tf_op jit(solution)/shard_map/pallas_call | solution.py:514
  45.6 0.0 copy-start.1
  45.6 0.7 copy-done.1
  46.3 26.1 %shard_map.142 = bf16[128,1024]{1,0:T(8,128)(2,1)} custom-call(bf16[128,1024]{1,0:T(8,128)(2,1)} %bitcast.7, bf16[512,256]{1,0:T(8,128)(2,1)} %copy-done.1, bf16[1024,1024]{1,0:T(8,128)(2,1)} %proj_hbm.1, f32[1,1024]{1,0:T(1,128)} %bitcast.14, bf16[1024,1024]{1,0:T(8,128)(2,1)} %in_hbm.1, bf16[1024,1024]{1,0:T(8,128)(2,1)} %out_hbm.1), custom_call_target="tpu_custom_call" | custom-call | tf_op jit(solution)/shard_map/pallas_call | solution.py:527
  72.4 0.0 copy-start.5
  72.5 1.0 %copy.26 = bf16[512,512]{0,1:T(8,128)(2,1)} copy(bf16[512,512]{1,0:T(8,128)(2,1)S(1)} %slice.3) | data formatting | bytes 1048576 | tf_op jit(solution)/shard_map/slice | solution.py:548
  73.5 0.0 copy-done.5
  73.5 0.7 copy.28
  (1 shorter events, 0.0 us)
Async XLA Ops:
  0.6 2.1 %copy-start = (bf16[1,128,1024]{2,1,0:T(8,128)(2,1)S(1)}, bf16[1,128,1024]{2,1,0:T(8,128)(2,1)}, u32[]{:S(2)}) copy-start(bf16[1,128,1024]{2,1,0:T(8,128)(2,1)} %param.13) | copy-start | bytes 786436
  0.6 1.8 %copy-start.6 = (bf16[1,256,2,4,64]{1,4,3,2,0:T(8,128)(2,1)S(1)}, bf16[1,256,2,4,64]{1,4,3,2,0:T(8,128)(2,1)}, u32[]{:S(2)}) copy-start(bf16[1,256,2,4,64]{1,4,3,2,0:T(8,128)(2,1)} %param.17) | copy-start | bytes 786436
  0.7 2.0 %copy-start.8 = (s32[8,2]{0,1:T(2,128)S(1)}, s32[8,2]{0,1:T(2,128)}, u32[]{:S(2)}) copy-start(s32[8,2]{0,1:T(2,128)} %param.19) | copy-start | bytes 196
  0.7 2.1 %copy-start.2 = (f32[1024]{0:T(1024)S(1)}, f32[1024]{0:T(1024)}, u32[]{:S(2)}) copy-start(f32[1024]{0:T(1024)} %param.14) | copy-start | bytes 12292
  0.7 2.1 %copy-start.4 = (s32[8]{0:T(128)S(1)}, s32[8]{0:T(128)}, u32[]{:S(2)}) copy-start(s32[8]{0:T(128)} %owner.1) | copy-start | bytes 100
  2.5 32.2 %copy-start.7 = (f32[32,4]{0,1:T(4,128)S(1)}, f32[32,4]{0,1:T(4,128)}, u32[]{:S(2)}) copy-start(f32[32,4]{0,1:T(4,128)} %param.16) | copy-start | bytes 1540
  2.5 32.3 %copy-start.9 = (s32[8,2]{0,1:T(2,128)S(1)}, s32[8,2]{0,1:T(2,128)}, u32[]{:S(2)}) copy-start(s32[8,2]{0,1:T(2,128)} %param.20) | copy-start | bytes 196
  2.5 32.3 %copy-start.3 = (s32[8,16]{1,0:T(8,128)S(1)}, s32[8,16]{1,0:T(8,128)}, u32[]{:S(2)}) copy-start(s32[8,16]{1,0:T(8,128)} %pages.1) | copy-start | bytes 1540
  45.6 0.7 copy-start.1
  72.4 1.1 %copy-start.5 = (bf16[128,1024]{1,0:T(8,128)(2,1)S(1)}, bf16[128,1024]{1,0:T(8,128)(2,1)}, u32[]{:S(2)}) copy-start(bf16[128,1024]{1,0:T(8,128)(2,1)} %shard_map.142) | copy-start | bytes 786436
